TPU v7x, 128 devices: a whole 4x4x4 slice. The times are simulated.
128 devices in a mesh: ctx: 8 (over z, core), tp: 16 (over y, x).
Axes of the slice: x: 4, y: 4, z: 4, core: 2. Of those that a mesh axis runs over, the one named last changes fastest.
Arguments:
- tokens: bfloat16 [16384, 4096], P(('ctx', 'tp')), may hold values from -45 to 45, as said below
- norm_gain: float32 [4096], replicated, may hold values from 0.1 to 1.9
- w_in: bfloat16 [4096, 3, 4096], P(None, None, 'tp'), may hold values from -0.09375 to 0.09375
- conv_w: float32 [7, 3, 4096], P(None, None, 'tp'), may hold values from -2.5 to 2.5
- decay_rate: float32 [16, 4096], P(None, 'tp'), may hold values from 1e-06 to 0.15, as said below
- residue: float32 [16, 4096], P(None, 'tp'), may hold values from -0.6 to 0.6, as said below
- skip_gain: float32 [4096], P('tp'), may hold values from -3 to 3
- w_out: bfloat16 [4096, 4096], P('tp'), may hold values from -0.09375 to 0.09375
Outputs:
- block_out: bfloat16 [16384, 4096], P(('ctx', 'tp'))
Inputs may be any that keep to these rules, and one draw needn't show every extreme that they name: `tokens`: activations entering the block. `decay_rate`: decay rates are positive. `residue`: residues of the modal filter.
All inputs are finite; a program needn't handle non-finite values.
Results may differ from a plain program's by a relative error of at most 0.024.
Values may be sent and summed in bfloat16 or wider, within the bound.
A program may use at most 192 MiB of HBM per device.

v0:
```python
import jax
import jax.numpy as jnp
from jax import lax
from jax.sharding import PartitionSpec as P

TAPS = 7
BLOCK = 128


epsilon = 1e-05
highest = lax.Precision.HIGHEST


def shifted(block, axis, distance):
    devices = range(lax.axis_size(axis))
    route = [(i - distance, i) for i in devices if i - distance in devices]
    return lax.ppermute(block, axis, route)


def entering(x, axis, combine, identity):
    count, place = (lax.axis_size(axis), lax.axis_index(axis))
    everything = jax.tree.map(
        lambda part, kind: lax.all_gather(part.astype(kind), axis), x, (jnp.bfloat16, jnp.bfloat16)
    )
    start = jax.tree.map(
        lambda part, zero: jnp.broadcast_to(jnp.asarray(zero, part.dtype), part.shape), x, identity
    )

    def hop(k, before):
        reached = k < place
        new = combine(
            before, jax.tree.map(lambda part, own: part[k].astype(own.dtype), everything, x)
        )
        return jax.tree.map(lambda a, b: jnp.where(reached, a, b), new, before)

    return lax.fori_loop(0, count, hop, start)


def normalize(tokens, norm_gain):
    floats = tokens.astype(jnp.float32)
    mean_square = jnp.mean(floats * floats, axis=1, keepdims=True)
    return (floats * lax.rsqrt(mean_square + epsilon) * norm_gain).astype(jnp.bfloat16)


def featurize(projected, tail_rows, conv_w):
    filter_taps = conv_w.reshape(TAPS, -1)
    extended = jnp.concatenate([tail_rows, projected], axis=-2).astype(jnp.float32)
    length = projected.shape[-2]
    summed = filter_taps[0] * extended[..., 0:length, :]
    for offset in range(1, TAPS):
        summed = summed + filter_taps[offset] * extended[..., offset : offset + length, :]
    return summed


def channel_tables(rates, residues):
    distance = jnp.arange(BLOCK, dtype=jnp.float32)
    powers = jnp.exp(-rates[:, :, None] * distance[None, None, :])
    impulse = jnp.sum(powers * residues[:, :, None], axis=1)
    positions = jnp.arange(BLOCK, dtype=jnp.int32)
    lag_rows = positions[:, None] - positions[None, :]
    toeplitz = jnp.where((lag_rows >= 0)[None], impulse[:, jnp.maximum(lag_rows, 0)], 0.0)
    end_power = jnp.exp(-rates[:, :, None] * (BLOCK - 1.0 - distance)[None, None, :])
    out_power = jnp.exp(-rates[:, :, None] * (distance + 1.0)[None, None, :]) * residues[:, :, None]
    return (toeplitz, end_power, out_power)


def combine_states(earlier, latter):
    return (earlier[0] * latter[0], latter[0] * earlier[1] + latter[1])


def to_channels(product):
    rows_all, channels = product.shape
    return product.T.reshape(channels, rows_all // BLOCK, BLOCK)


def block_states(grouped, rates, end_power):
    block_ends = jnp.einsum("cns,cbs->cnb", end_power, grouped, precision=highest)
    block_decay = jnp.broadcast_to(jnp.exp(-rates * BLOCK)[:, :, None], block_ends.shape)
    return lax.associative_scan(combine_states, (block_decay, block_ends), axis=2)[1]


def long_mix(grouped, inclusive, carried, rates, toeplitz, out_power):
    channels, blocks, _ = grouped.shape
    within = jnp.einsum("cts,cbs->cbt", toeplitz, grouped, precision=highest)
    starts = jnp.concatenate([jnp.zeros_like(inclusive[:, :, :1]), inclusive[:, :, :-1]], axis=2)
    offsets = jnp.arange(blocks, dtype=jnp.float32) * BLOCK
    starts = starts + jnp.exp(-rates[:, :, None] * offsets[None, None, :]) * carried[:, :, None]
    from_state = jnp.einsum("cnt,cnb->cbt", out_power, starts, precision=highest)
    return (within + from_state).reshape(channels, blocks * BLOCK).T


def split_streams(features, channels):
    queries = features[..., :channels]
    product = features[..., channels : 2 * channels] * features[..., 2 * channels :]
    return (queries, product)


def shards(tokens, norm_gain, w_in, conv_w, decay_rate, residue, skip_gain, w_out):
    channels = w_in.shape[2]
    flat_in = w_in.reshape(w_in.shape[0], 3 * channels)
    normed = normalize(tokens, norm_gain)
    projected = jnp.dot(
        lax.all_gather(normed, "tp", axis=0, tiled=True),
        flat_in,
        preferred_element_type=jnp.float32,
    ).astype(jnp.bfloat16)
    rows_all = projected.shape[0]
    margin = TAPS - 1
    rates = decay_rate.T
    residues = residue.T
    toeplitz, end_power, out_power = channel_tables(rates, residues)
    tail_rows = shifted(projected[rows_all - margin :], "ctx", 1)
    features = featurize(projected, tail_rows, conv_w)
    queries, product = split_streams(features, channels)
    grouped = to_channels(product)
    inclusive = block_states(grouped, rates, end_power)
    shard_decay = jnp.exp(-rates * rows_all)
    carried = entering(
        (shard_decay, inclusive[:, :, -1]),
        "ctx",
        combine_states,
        (jnp.ones_like(shard_decay), jnp.zeros_like(shard_decay)),
    )[1]
    mixed_long = long_mix(grouped, inclusive, carried, rates, toeplitz, out_power)
    gated = (queries * (mixed_long + skip_gain * product)).astype(jnp.bfloat16)
    summed = lax.psum_scatter(
        jnp.dot(gated, w_out, preferred_element_type=jnp.float32).astype(jnp.bfloat16),
        "tp",
        scatter_dimension=0,
        tiled=True,
    ).astype(jnp.float32)
    return (tokens.astype(jnp.float32) + summed).astype(jnp.bfloat16)


def solution(mesh):
    return jax.shard_map(
        shards,
        mesh=mesh,
        in_specs=(
            P(("ctx", "tp"), None),
            P(),
            P(None, None, "tp"),
            P(None, None, "tp"),
            P(None, "tp"),
            P(None, "tp"),
            P("tp"),
            P("tp", None),
        ),
        out_specs=P(("ctx", "tp"), None),
        check_vma=False,
    )
```

profile of v0, /device:TPU:1, one launch (start us, length us, event | category | flops | bytes accessed | tf_op | source)
XLA Modules:
  0.0 507.2 jit_solution(3578361440260742817)
XLA Ops:
  10.9 8.8 %copy.71 = bf16[4096,3,256]{0,2,1:T(8,128)(2,1)} copy(bf16[4096,3,256]{2,0,1:T(8,128)(2,1)} %param.12) | data formatting | bytes 12582912 | tf_op args[2]
  24.0 101.3 %all-gather.4.cloned.1.call-done = bf16[2048,4096]{1,0:T(8,128)(2,1)} async-done(((bf16[128,4096]{1,0:T(8,128)(2,1)}), bf16[2048,4096]{1,0:T(8,128)(2,1)}) %all-gather.4.cloned.1.call-update) | async-done | bytes 16777232 | tf_op jit(solution)/shard_map/all_gather | solution.py:103
  125.3 18.2 %convolution_convert_fusion.1 = bf16[2048,768]{1,0:T(8,128)(2,1)S(1)} fusion(bf16[2048,4096]{1,0:T(8,128)(2,1)} %all-gather.4.cloned.1.call-done, bf16[4096,768]{0,1:T(8,128)(2,1)} %bitcast.65), kind=kOutput, calls=%fused_computation.23 | convolution fusion | flops 12886474752 | bytes 26214400 | tf_op jit(solution)/shard_map/dot_general | solution.py:102
  145.1 3.8 collective-permute-start
  148.9 12.1 %all-gather = bf16[2048,16]{0,1:T(8,128)(2,1)S(1)} all-gather(bf16[256,16]{0,1:T(8,128)(2,1)S(1)} %get-tuple-element.164), channel_id=2, replica_groups=mesh['ctx'=8,'tp'=16] {'ctx'}, dimensions={0}, use_global_device_ids=true | all-gather | bytes 73728 | tf_op jit(solution)/shard_map/all_gather | solution.py:23
  161.2 61.7 %gather_fusion = f32[16384,256]{1,0:T(8,128)} fusion(f32[256,128]{0,1:T(8,128)S(1)} %copy.74, s32[16384]{0:T(1024)S(1)} %bitcast_clamp_fusion), kind=kCustom, calls=%fused_computation | custom fusion | bytes 33619968 | tf_op jit(solution)/shard_map/gather | solution.py:61
  222.9 18.0 %copy.75 = f32[128,128,256]{1,0,2:T(8,128)} copy(f32[128,128,256]{2,1,0:T(8,128)} %bitcast.63) | data formatting | bytes 33554432 | tf_op jit(solution)/shard_map/gather | solution.py:61
  241.5 5.2 %maximum_convert_fusion = f32[2054,768]{1,0:T(8,128)} fusion(bf16[2048,768]{1,0:T(8,128)(2,1)} %copy-done.3, bf16[6,768]{1,0:T(8,128)(2,1)S(1)} %collective-permute-done), kind=kLoop, calls=%fused_computation.24 | loop fusion | flops 6309888 | bytes 9464832 | tf_op jit(solution)/shard_map/convert_element_type | solution.py:47
  246.7 19.1 %fusion.6 = f32[2048,768]{1,0:T(8,128)} fusion(f32[2054,768]{1,0:T(8,128)} %maximum_convert_fusion, f32[768]{0:T(1024)S(1)} %mul.255, f32[768]{0:T(1024)S(1)} %mul.252, f32[768]{0:T(1024)S(1)} %mul.249, f32[768]{0:T(1024)S(1)} %mul.246, f32[768]{0:T(1024)S(1)} %mul.243, f32[768]{0:T(1024)S(1)} %mul.240, f32[768]{0:T(1024)S(1)} %mul.232), kind=kLoop, calls=%fused_computation.11 | loop fusion | flops 20447232 | bytes 50353152 | tf_op jit(solution)/shard_map/add | solution.py:51
  265.8 3.8 slice_multiply_fusion.7
  269.6 3.1 copy.76
  272.7 6.5 %fusion.21 = f32[256,16,16]{1,2,0:T(8,128)} fusion(f32[256,16,128]{2,1,0:T(8,128)} %copy.76, f32[128]{0:T(128)S(1)} %iota_subtract_fusion, f32[256,16]{1,0:T(8,128)S(1)} %copy.72), kind=kOutput, calls=%fused_computation.40 | convolution fusion | flops 101187584 | bytes 2376192 | tf_op jit(solution)/shard_map/cns,cbs->cnb/dot_general | solution.py:77
  279.2 6.2 %slice.169 = f32[256,16,8]{1,2,0:T(8,128)} slice(f32[256,16,16]{1,2,0:T(8,128)} %fusion.21), slice={[0:256:1], [0:16:1], [1:16:2]} | slice | bytes 262144 | tf_op jit(solution)/shard_map/slice | solution.py:79
  285.4 5.0 slice.168
  298.0 5.1 slice.188
  308.7 3.1 pad.33
  311.8 3.1 pad.67
  318.0 13.0 %all-gather.1 = bf16[2048,16,1]{0,1,2:T(8,128)(2,1)S(1)} all-gather(bf16[256,16,1]{0,1,2:T(8,128)(2,1)S(1)} %add_convert_fusion), channel_id=3, replica_groups=mesh['ctx'=8,'tp'=16] {'ctx'}, dimensions={0}, use_global_device_ids=true | all-gather | bytes 73728 | tf_op jit(solution)/shard_map/all_gather | solution.py:23
  331.0 5.7 %while.14 = (s32[]{:T(128)}, f32[256,16]{0,1:T(8,128)S(1)}, s32[]{:T(128)}, bf16[8,256,16]{1,2,0:T(8,128)(2,1)}, bf16[8,256,16]{1,2,0:T(8,128)(2,1)S(1)}, /*index=5*/s32[]{:T(128)}, s32[]{:T(128)}) while((s32[]{:T(128)}, f32[256,16]{0,1:T(8,128)S(1)}, s32[]{:T(128)}, bf16[8,256,16]{1,2,0:T(8,128)(2,1)}, ...), condition=%wide.region_3.4_spmd.clone, body=%wide.region_2.3_spmd.clone.sunk | while | flops 24580 | bytes 49261 | solution.py:36
  340.9 28.9 %fusion.1 = f32[256,16,128]{2,1,0:T(8,128)S(1)} fusion(f32[256,16,128]{2,1,0:T(8,128)} %copy.76, f32[128,128,256]{1,0,2:T(8,128)} %copy.75, pred[128,128]{1,0:T(8,128)(4,1)S(1)} %copy-done.7), kind=kOutput, calls=%fused_computation.4 | convolution fusion | flops 809500672 | bytes 20987904 | tf_op jit(solution)/shard_map/cts,cbs->cbt/dot_general | solution.py:84
  369.8 4.1 fusion.24
  376.9 4.1 fusion.16
  381.0 8.1 %convolution_convert_fusion = bf16[2048,4096]{1,0:T(8,128)(2,1)} fusion(bf16[2048,256]{1,0:T(8,128)(2,1)S(1)} %fusion.16, bf16[256,4096]{1,0:T(8,128)(2,1)S(1)} %copy-done), kind=kOutput, calls=%fused_computation.7 | convolution fusion | flops 4303355904 | bytes 19922944 | tf_op jit(solution)/shard_map/dot_general | solution.py:127
  389.1 108.8 %reduce-scatter.2.cloned.1.call-done = bf16[128,4096]{1,0:T(8,128)(2,1)} async-done(((bf16[2048,4096]{1,0:T(8,128)(2,1)}), bf16[128,4096]{1,0:T(8,128)(2,1)}) %reduce-scatter.2.cloned.1.call-update) | async-done | bytes 1048592 | tf_op jit(solution)/shard_map/reduce_scatter | solution.py:126
  (96 shorter events, 42.5 us)
Async XLA Ops:
  6.5 374.4 %copy-start = (bf16[256,4096]{1,0:T(8,128)(2,1)S(1)}, bf16[256,4096]{1,0:T(8,128)(2,1)}, u32[]{:S(2)}) copy-start(bf16[256,4096]{1,0:T(8,128)(2,1)} %param.17) | copy-start | bytes 6291460
  6.5 118.8 %all-gather.4.cloned.1.call-start = ((), (), s32[]{:S(2)}) async-start(), calls=%async_computation.1 | async-start | bytes 17825792 | tf_op jit(solution)/shard_map/all_gather | solution.py:103
  10.8 8.9 %copy-start.10 = (f32[16,256]{1,0:T(8,128)S(1)}, f32[16,256]{1,0:T(8,128)}, u32[]{:S(2)}) copy-start(f32[16,256]{1,0:T(8,128)} %param.15) | copy-start | bytes 49156
  10.8 9.0 %copy-start.6 = (f32[16,256]{1,0:T(8,128)S(1)}, f32[16,256]{1,0:T(8,128)}, u32[]{:S(2)}) copy-start(f32[16,256]{1,0:T(8,128)} %param.14) | copy-start | bytes 49156
  10.8 10.8 %copy-start.9 = (f32[7,3,256]{2,0,1:T(8,128)S(1)}, f32[7,3,256]{2,0,1:T(8,128)}, u32[]{:S(2)}) copy-start(f32[7,3,256]{2,0,1:T(8,128)} %param.13) | copy-start | bytes 64516
  10.8 487.1 %reduce-scatter.2.cloned.1.call-start = ((), (), s32[]{:S(2)}) async-start(), calls=%async_computation.2 | async-start | bytes 17825792 | tf_op jit(solution)/shard_map/reduce_scatter | solution.py:126
  19.8 123.7 %copy-start.4 = (f32[256,16]{1,0:T(8,128)}, f32[256,16]{1,0:T(8,128)S(1)}, u32[]{:S(2)}) copy-start(f32[256,16]{1,0:T(8,128)S(1)} %copy.73) | copy-start | bytes 49156
  19.8 123.7 %copy-start.8 = (f32[256,16]{0,1:T(8,128)}, f32[256,16]{0,1:T(8,128)S(1)}, u32[]{:S(2)}) copy-start(f32[256,16]{0,1:T(8,128)S(1)} %negate_bitcast_fusion) | copy-start | bytes 49156
  143.5 1.6 copy-start.3
  145.1 96.4 %collective-permute-start = (bf16[6,768]{1,0:T(8,128)(2,1)S(1)}, bf16[6,768]{1,0:T(8,128)(2,1)S(1)}, u32[]{:S(2)}, u32[]{:S(2)}) collective-permute-start(bf16[6,768]{1,0:T(8,128)(2,1)S(1)} %slice.193), channel_id=1, source_target_pairs={{0,16},{16,32},{32,48},{48,64},{64,80},{80,96},{96,112},{1,17},{17... | collective-permute-start | bytes 27656 | tf_op jit(solution)/shard_map/ppermute | solution.py:17
  315.0 26.0 %copy-start.7 = (pred[128,128]{1,0:T(8,128)(4,1)S(1)}, pred[128,128]{1,0:T(8,128)(4,1)}, u32[]{:S(2)}) copy-start(pred[128,128]{1,0:T(8,128)(4,1)} %subtract_compare_fusion) | copy-start | bytes 49156
  340.9 28.9 %copy-start.2 = (f32[256,16,16]{1,2,0:T(8,128)S(1)}, f32[256,16,16]{1,2,0:T(8,128)}, u32[]{:S(2)}) copy-start(f32[256,16,16]{1,2,0:T(8,128)} %copy.84) | copy-start | bytes 786436
  340.9 28.9 %copy-start.5 = (f32[256,16]{1,0:T(8,128)S(1)}, f32[256,16]{1,0:T(8,128)}, u32[]{:S(2)}) copy-start(f32[256,16]{1,0:T(8,128)} %copy-done.4) | copy-start | bytes 49156
  340.9 28.9 %copy-start.12 = (f32[128]{0:T(128)S(1)}, f32[128]{0:T(128)}, u32[]{:S(2)}) copy-start(f32[128]{0:T(128)} %iota_add_fusion) | copy-start | bytes 1540
  373.9 3.0 copy-start.11
  389.1 108.8 %copy-start.1 = (bf16[128,4096]{1,0:T(8,128)(2,1)S(1)}, bf16[128,4096]{1,0:T(8,128)(2,1)}, u32[]{:S(2)}) copy-start(bf16[128,4096]{1,0:T(8,128)(2,1)} %param.10) | copy-start | bytes 3145732
Sparse Core Ops, SparseCore 0:
  10.9 114.3 all-gather.3
  389.2 108.6 reduce-scatter.1
where the time goes:
time: 509 us; the launch traced here: 507 us
  waiting for transfers between devices  210 us (41%)
  local copies, waits for them, and re-layouts  130 us (26%)
  matrix products  65.7 us (13%)
  other arithmetic  58.7 us (12%)
  blocking collectives  25.1 us (5%)
  between operations  13.7 us (3%)
    reduce_scatter x1, waiting for transfers between devices, shards(): lax.psum_scatter(jnp.dot(gated, w_out, preferred_element_type=jnp.float32...  109 us
    all_gather x1, waiting for transfers between devices, shards(): lax.all_gather(normed, 'tp', axis=0, tiled=True)  101 us
    gather x2, local copies, waits for them, and re-layouts, channel_tables(): impulse[:, jnp.maximum(lag_rows, 0)]  79.7 us
    dot_general x1, matrix products, long_mix(): within = jnp.einsum('cts,cbs->cbt', toeplitz, grouped, precision=highest)  28.9 us
    all_gather x2, blocking collectives, entering(): lax.all_gather(part.astype(kind), axis)  25.1 us
    add x1, other arithmetic, featurize(): summed + filter_taps[offset] * extended[..., offset:offset + length, :]  19.1 us
    slice x5, local copies, waits for them, and re-layouts, block_states(): lax.associative_scan(combine_states, (block_decay, block_ends), axis=2)[1]  18.8 us
    dot_general x1, matrix products, shards(): jnp.dot(lax.all_gather(normed, 'tp', axis=0, tiled=True), flat_in, prefer...  18.2 us
  transfers between devices with their start and end apart: 3, of which 2 were waited for; matrix products, arithmetic and copies ran while one was open for 18% of the time, Pallas kernels for 0%

commit v1 on v0

v1 whole, which is shorter than its diff:
```python
import functools

import jax
import jax.numpy as jnp
from jax import lax
from jax.experimental import pallas as pl
from jax.experimental.pallas import tpu as pltpu
from jax.sharding import PartitionSpec as P

TAPS = 7
POLES = 16
D = 4096
CH = 256
ROWS = 128
TEAM = 512
HALO = 16
SEGS = 8
STEPS = TEAM // SEGS
LEAD = 8
EPS = 1e-05
MESH = pl.DeviceIdType.MESH
NSEM = 96
OUT_COLS = 512
OUT_PARTS = D // OUT_COLS

f32 = jnp.float32
bf16 = jnp.bfloat16


def tree_sum(parts):
    parts = list(parts)
    while len(parts) > 1:
        parts = [
            parts[i] + parts[i + 1] if i + 1 < len(parts) else parts[i]
            for i in range(0, len(parts), 2)
        ]
    return parts[0]


def kernel(
    tok_h, gain, win_h, conv, decay, res, skip, wout_h,
    out_h,
    tok, lhs, w_all, w_out, par, proj, prod, q_all, y_all, pref, gbuf, gated,
    stage, landed, ends, totals, carry, outv, send, recv, osend, orecv, local,
):
    ctx = lax.axis_index("ctx")
    tp = lax.axis_index("tp")
    z, k = ctx // 2, ctx % 2
    y, x = tp // 4, tp % 4

    def dev(dz=0, dk=0, dy=0, dx=0):
        return (
            ((z + dz) % 4) * 2 + (k + dk) % 2,
            ((y + dy) % 4) * 4 + (x + dx) % 4,
        )

    place = ctx * 4 + y
    after, before = (place + 1) % 32, (place + 31) % 32
    dev_after = (after // 4, (after % 4) * 4 + x)
    dev_before = (before // 4, (before % 4) * 4 + x)

    count = [0]
    started = []

    def remote(src, dst, device):
        i = count[0]
        count[0] += 1
        return pltpu.make_async_remote_copy(
            src_ref=src, dst_ref=dst, send_sem=send.at[i], recv_sem=recv.at[i],
            device_id=device, device_id_type=MESH,
        )

    def go(copy):
        copy.start()
        started.append(copy)
        return copy

    gm, gp, g2 = (y + 3) % 4, (y + 1) % 4, (y + 2) % 4

    copy_tok = pltpu.make_async_copy(tok_h, tok, local.at[0])
    copy_win = pltpu.make_async_copy(win_h, w_all.at[y], local.at[1])
    copy_out = pltpu.make_async_copy(
        wout_h, w_out.at[pl.ds(pl.multiple_of(y * CH, CH), CH)], local.at[2]
    )
    copy_tok.start()
    copy_win.start()
    copy_out.start()

    for s in range(3):
        par[y, s * 8:s * 8 + TAPS, :] = conv[s]
    par[y, 24:40, :] = decay[...]
    par[y, 40:56, :] = res[...]
    par[y, 56:57, :] = skip[...]

    partners = [dev(dx=1), dev(dx=2), dev(dx=3), dev(dy=1), dev(dy=2), dev(dy=3)]
    partners += [dev(dz=a, dk=b) for a in range(4) for b in range(2) if a or b]
    partners += [dev_after, dev_before]
    barrier = pltpu.get_barrier_semaphore()
    for d in partners:
        pl.semaphore_signal(barrier, inc=1, device_id=d, device_id_type=MESH)
    pl.semaphore_wait(barrier, len(partners))

    YP, YM, ZP, ZM, SIB = dev(dy=1), dev(dy=3), dev(dz=1), dev(dz=3), dev(dk=1)
    XP, XM = dev(dx=1), dev(dx=3)

    def rows_in(zz, n=512):
        return pl.ds(pl.multiple_of(k * 2048 + zz * n, n), n)

    def piece(kind, g, zz, half):
        if kind == "in":
            return w_all.at[g, 1 + half, rows_in(zz)]
        at = g * CH + k * 128 + zz * 32 + half * 16
        return w_out.at[pl.ds(pl.multiple_of(at, 16), 16)]

    def own_piece(kind, half):
        if kind == "in":
            return win_h.at[1 + half, rows_in(z)]
        at = k * 128 + z * 32 + half * 16
        return wout_h.at[pl.ds(pl.multiple_of(at, 16), 16)]

    class Weights:
        def __init__(self, kind):
            self.kind = kind
            own = lambda h, d: remote(own_piece(kind, h), piece(kind, y, z, h), d)
            self.to_p = [own(h, YP) for h in range(2)]
            self.to_m = [own(h, YM) for h in range(2)]
            self.fwd_p = remote(piece(kind, gm, z, 0), piece(kind, gm, z, 0), YP)
            self.fwd_m = remote(piece(kind, gp, z, 1), piece(kind, gp, z, 1), YM)
            same = lambda g, zz, h, d: remote(piece(kind, g, zz, h), piece(kind, g, zz, h), d)
            self.z_p, self.z_m, self.zf_p, self.zf_m = {}, {}, {}, {}
            for name, g in (("m", gm), ("p", gp), ("2", g2)):
                self.z_p[name] = [same(g, z, h, ZP) for h in range(2)]
                self.z_m[name] = [same(g, z, h, ZM) for h in range(2)]
                self.zf_p[name] = same(g, (z + 3) % 4, 0, ZP)
                self.zf_m[name] = same(g, (z + 1) % 4, 1, ZM)

        def start(self):
            for h in (0, 1):
                go(self.to_p[h] if h == 0 else self.to_m[h])
                go(self.to_m[h] if h == 0 else self.to_p[h])

        def spread(self, name, h):
            go(self.z_p[name][h])
            go(self.z_m[name][h])

        def along_y(self):
            self.to_p[0].wait_recv()
            go(self.fwd_p)
            self.spread("m", 0)
            self.to_m[0].wait_recv()
            self.spread("p", 0)
            self.to_m[1].wait_recv()
            go(self.fwd_m)
            self.spread("p", 1)
            self.to_p[1].wait_recv()
            self.spread("m", 1)

        def along_y2(self):
            self.fwd_p.wait_recv()
            self.spread("2", 0)
            self.fwd_m.wait_recv()
            self.spread("2", 1)

        def forward_z(self, name):
            self.z_p[name][0].wait_recv()
            go(self.zf_p[name])
            self.z_m[name][1].wait_recv()
            go(self.zf_m[name])

        def finish(self, name):
            self.z_m[name][0].wait_recv()
            self.z_p[name][1].wait_recv()
            self.zf_p[name].wait_recv()
            self.zf_m[name].wait_recv()

    wi = Weights("in")
    wo = Weights("out")

    def q_rows(h):
        return pl.ds(pl.multiple_of(k * 2048 + h * 1024, 1024), 1024)

    def q_own(h, d):
        return remote(win_h.at[0, q_rows(h)], w_all.at[y, 0, q_rows(h)], d)

    q_p = [q_own(h, YP) for h in range(2)]
    q_m = [q_own(h, YM) for h in range(2)]
    q_fp = remote(w_all.at[gm, 0, q_rows(0)], w_all.at[gm, 0, q_rows(0)], YP)
    q_fm = remote(w_all.at[gp, 0, q_rows(1)], w_all.at[gp, 0, q_rows(1)], YM)

    half = pl.ds(pl.multiple_of(k * 2048, 2048), 2048)
    push = {}
    push_out = {}
    for name, g in (("m", gm), ("p", gp), ("2", g2)):
        push[name] = [remote(w_all.at[g, s, half], w_all.at[g, s, half], SIB) for s in range(3)]
        o_half = pl.ds(pl.multiple_of(g * CH + k * 128, 128), 128)
        push_out[name] = remote(w_out.at[o_half], w_out.at[o_half], SIB)

    par_copies = [remote(par.at[y], par.at[y], dev(dy=d)) for d in (1, 3, 2)]

    def x_rows(who, h):
        return lhs.at[pl.ds(pl.multiple_of(HALO + who * ROWS + h * 64, 16), 64)]

    x_p = [remote(x_rows(x, h), x_rows(x, h), XP) for h in range(2)]
    x_m = [remote(x_rows(x, h), x_rows(x, h), XM) for h in range(2)]
    xm, xp = (x + 3) % 4, (x + 1) % 4
    x_fp = remote(x_rows(xm, 0), x_rows(xm, 0), XP)
    x_fm = remote(x_rows(xp, 1), x_rows(xp, 1), XM)
    halo_copy = remote(lhs.at[pl.ds(TEAM, HALO)], lhs.at[pl.ds(0, HALO)], dev_after)

    wi.start()
    copy_tok.wait()

    def norm_rows(i, c):
        v = tok[pl.ds(pl.multiple_of(i * 16, 16), 16), :].astype(f32)
        ms = jnp.sum(v * v, axis=1, keepdims=True) * (1.0 / D)
        v = (v * lax.rsqrt(ms + EPS) * gain[...]).astype(bf16)
        lhs[pl.ds(pl.multiple_of(HALO + x * ROWS + i * 16, 16), 16), :] = v
        return c

    lax.fori_loop(0, 4, norm_rows, 0)
    go(x_p[0])
    go(x_m[0])
    lax.fori_loop(4, 8, norm_rows, 0)
    go(x_m[1])
    go(x_p[1])
    for c in par_copies:
        go(c)
    go(q_p[0])
    go(q_m[1])
    go(q_m[0])
    go(q_p[1])

    wi.along_y()
    wi.along_y2()
    x_p[0].wait_recv()
    go(x_fp)
    x_m[1].wait_recv()
    go(x_fm)
    wi.forward_z("m")
    wi.forward_z("p")
    q_p[0].wait_recv()
    go(q_fp)
    q_m[1].wait_recv()
    go(q_fm)
    wo.start()
    x_p[1].wait_recv()
    x_m[0].wait_recv()
    x_fp.wait_recv()
    x_fm.wait_recv()
    go(halo_copy)
    for c in par_copies:
        c.wait_recv()
    copy_win.wait()
    halo_copy.wait_recv()

    @pl.when(place == 0)
    def _():
        lhs[0:HALO, :] = jnp.zeros((HALO, D), bf16)

    sub = lax.broadcasted_iota(jnp.int32, (SEGS, 128), 0)

    def project(g):
        for s in range(3):
            def k_step(j, acc):
                at = pl.ds(pl.multiple_of(j * 1024, 1024), 1024)
                return acc + jnp.dot(lhs[:, at], w_all[g, s, at, :], preferred_element_type=f32)

            acc = lax.fori_loop(0, 4, k_step, jnp.zeros((HALO + TEAM, CH), f32))
            acc = acc.astype(bf16).astype(f32)
            for h in range(2):
                part = acc[:, h * 128:(h + 1) * 128]
                for seg in range(SEGS):
                    proj[s, h, pl.ds(LEAD * SEGS + seg, STEPS, stride=SEGS), :] = part[
                        HALO + seg * STEPS:HALO + (seg + 1) * STEPS
                    ]
                for j in range(1, TAPS):
                    last = proj[s, h, pl.ds((LEAD + STEPS - j) * SEGS, SEGS), :]
                    first = jnp.broadcast_to(part[HALO - j:HALO - j + 1], (SEGS, 128))
                    proj[s, h, pl.ds((LEAD - j) * SEGS, SEGS), :] = jnp.where(
                        sub == 0, first, pltpu.roll(last, 1, 0)
                    )

    def featurize(g):
        for h in range(2):
            lanes = pl.ds(h * 128, 128)
            taps = [par[g, s * 8:s * 8 + 8, lanes] for s in range(3)]

            def steps(i, c):
                feats = []
                for s in range(3):
                    at = pl.multiple_of((i * 8 + LEAD - TAPS + 1) * SEGS, SEGS)
                    rows = proj[s, h, pl.ds(at, 14 * SEGS), :]
                    feats.append(tree_sum([
                        taps[s][j:j + 1] * rows[j * SEGS:j * SEGS + 64] for j in range(TAPS)
                    ]))
                to = pl.ds(pl.multiple_of(i * 64, 64), 64)
                q_all[g, h, to, :] = feats[0]
                prod[h, to, :] = feats[1] * feats[2]
                return c

            lax.fori_loop(0, STEPS // 8, steps, 0)

    def scan(g):
        for h in range(2):
            lanes = pl.ds(h * 128, 128)
            rate = par[g, 24:40, lanes]
            rs = par[g, 40:56, lanes]
            wide = lambda v: jnp.broadcast_to(v, (SEGS, 128))
            power = jnp.exp(-rate)
            a = [wide(power[n:n + 1]) for n in range(POLES)]
            r = [wide(rs[n:n + 1]) for n in range(POLES)]
            direct = wide(par[g, 56:57, lanes])

            def steps(i, states):
                for u in range(4):
                    at = pl.ds(pl.multiple_of((i * 4 + u) * SEGS, SEGS), SEGS)
                    v = prod[h, at, :]
                    states = [a[n] * states[n] + r[n] * v for n in range(POLES)]
                    y_all[g, h, at, :] = tree_sum(states) + direct * v
                return states

            states = lax.fori_loop(
                0, STEPS // 4, steps, [jnp.zeros((SEGS, 128), f32)] * POLES
            )
            for n in range(POLES):
                v = states[n]
                for dist in (1, 2, 4):
                    hop = jnp.exp(rate[n:n + 1] * (-1.0 * STEPS * dist))
                    v = v + hop * jnp.where(sub >= dist, pltpu.roll(v, dist, 0), 0.0)
                pref[g, h, n] = jnp.where(sub >= 1, pltpu.roll(v, 1, 0), 0.0)
                ends[y, g, h, n:n + 1, :] = v[SEGS - 1:SEGS]

    def weights_ready(name):
        wi.finish(name)
        go(push[name][1])
        go(push[name][2])

    def q_ready(name):
        if name == "m":
            q_p[1].wait_recv()
        elif name == "p":
            q_m[0].wait_recv()
        else:
            q_fp.wait_recv()
            q_fm.wait_recv()
        go(push[name][0])

    def group(i, c):
        @pl.when(i == 1)
        def _():
            wi.forward_z("2")
            q_ready("m")
            q_ready("p")
            weights_ready("m")
            wo.along_y()
            weights_ready("p")
            for c in push["m"]:
                c.wait_recv()

        @pl.when(i == 2)
        def _():
            wo.along_y2()
            q_ready("2")
            for c in push["p"]:
                c.wait_recv()

        @pl.when(i == 3)
        def _():
            weights_ready("2")
            wo.forward_z("m")
            wo.forward_z("p")
            for c in push["2"]:
                c.wait_recv()

        turn = jnp.where(i == 0, 0, jnp.where(i == 1, 3, jnp.where(i == 2, 1, 2)))
        g = (y + turn) % 4
        project(g)
        featurize(g)
        scan(g)
        return c

    lax.fori_loop(0, 4, group, 0)

    end_copies = [remote(ends.at[y], ends.at[y], dev(dy=d)) for d in (1, 3, 2)]
    for c in end_copies:
        go(c)
    wo.forward_z("2")
    for c in end_copies:
        c.wait_recv()
    for g in range(4):
        for h in range(2):
            rate = par[g, 24:40, h * 128:(h + 1) * 128]
            hop = jnp.exp(rate * (-1.0 * TEAM))
            total = ends[0, g, h]
            for yy in range(1, 4):
                total = hop * total + ends[yy, g, h]
            totals[ctx, g, h] = total
    total_copies = [
        remote(totals.at[ctx], totals.at[ctx], dev(dz=a, dk=b))
        for a in range(4) for b in range(2) if a or b
    ]
    for c in total_copies:
        go(c)
    for name in ("m", "p", "2"):
        wo.finish(name)
        go(push_out[name])
    for c in total_copies:
        c.wait_recv()

    for g in range(4):
        for h in range(2):
            rate = par[g, 24:40, h * 128:(h + 1) * 128]
            far = jnp.exp(rate * (-4.0 * TEAM))
            near = jnp.exp(rate * (-1.0 * TEAM))
            v = jnp.zeros((POLES, 128), f32)
            for cc in range(7):
                v = jnp.where(cc < ctx, far * v + totals[cc, g, h], v)
            for yy in range(3):
                v = jnp.where(yy < y, near * v + ends[yy, g, h], v)
            carry[g, h] = v

    segs = sub.astype(f32)

    def correct(g, c):
        for h in range(2):
            lanes = pl.ds(h * 128, 128)
            rate = par[g, 24:40, lanes]
            power = jnp.exp(-rate)
            wide = lambda v: jnp.broadcast_to(v, (SEGS, 128))
            a = [wide(power[n:n + 1]) for n in range(POLES)]
            begin = carry[g, h]
            states = []
            for n in range(POLES):
                seg_power = jnp.exp(wide(rate[n:n + 1]) * (segs * (-1.0 * STEPS)))
                states.append(pref[g, h, n] + seg_power * wide(begin[n:n + 1]))

            def steps(i, states):
                for u in range(4):
                    at = pl.ds(pl.multiple_of((i * 4 + u) * SEGS, SEGS), SEGS)
                    states = [a[n] * states[n] for n in range(POLES)]
                    gbuf[h, at, :] = q_all[g, h, at, :] * (y_all[g, h, at, :] + tree_sum(states))
                return states

            lax.fori_loop(0, STEPS // 4, steps, states)
            for seg in range(SEGS):
                gated[g, seg * STEPS:(seg + 1) * STEPS, h * 128:(h + 1) * 128] = gbuf[
                    h, pl.ds(seg, STEPS, stride=SEGS), :
                ].astype(bf16)
        return c

    lax.fori_loop(0, 4, correct, 0)

    copy_out.wait()
    for name in ("m", "p", "2"):
        push_out[name].wait_recv()

    def part_copy(n, d):
        cols = pl.ds(pl.multiple_of(n * OUT_COLS, OUT_COLS), OUT_COLS)
        to = (x + d) % 4
        rows = pl.ds(pl.multiple_of(to * ROWS, ROWS), ROWS)
        return pltpu.make_async_remote_copy(
            src_ref=stage.at[rows, cols], dst_ref=landed.at[x, :, cols],
            send_sem=osend.at[d - 1, n], recv_sem=orecv.at[d - 1, n],
            device_id=dev(dx=d), device_id_type=MESH,
        )

    def out_part(n, c):
        cols = pl.ds(pl.multiple_of(n * OUT_COLS, OUT_COLS), OUT_COLS)
        acc = jnp.zeros((TEAM, OUT_COLS), f32)
        for g in range(4):
            acc = acc + jnp.dot(gated[g], w_out[g * CH:(g + 1) * CH, cols], preferred_element_type=f32)
        stage[:, cols] = acc.astype(bf16)
        for d in (2, 1, 3):
            part_copy(n, d).start()
        return c

    lax.fori_loop(0, OUT_PARTS, out_part, 0)

    def add_part(n, c):
        cols = pl.ds(pl.multiple_of(n * OUT_COLS, OUT_COLS), OUT_COLS)
        for d in (1, 2, 3):
            part_copy(n, d).wait_recv()
        total = tok[:, cols].astype(f32) + stage[
            pl.ds(pl.multiple_of(x * ROWS, ROWS), ROWS), cols
        ].astype(f32)
        for d in (1, 2, 3):
            total = total + landed[(x + d) % 4, :, cols].astype(f32)
        outv[:, cols] = total.astype(bf16)
        return c

    lax.fori_loop(0, OUT_PARTS, add_part, 0)
    copy_res = pltpu.make_async_copy(outv, out_h, local.at[3])
    copy_res.start()

    def sent_part(n, c):
        for d in (1, 2, 3):
            part_copy(n, d).wait_send()
        return c

    lax.fori_loop(0, OUT_PARTS, sent_part, 0)
    for c in started:
        c.wait_send()
    copy_res.wait()


def shards(tokens, norm_gain, w_in, conv_w, decay_rate, residue, skip_gain, w_out):
    anywhere = pl.BlockSpec(memory_space=pl.ANY)
    inside = pl.BlockSpec(memory_space=pltpu.VMEM)
    vmem = pltpu.VMEM
    return pl.pallas_call(
        kernel,
        out_shape=jax.ShapeDtypeStruct(tokens.shape, tokens.dtype),
        in_specs=[anywhere, inside, anywhere, inside, inside, inside, inside, anywhere],
        out_specs=anywhere,
        scratch_shapes=[
            vmem((ROWS, D), bf16),
            vmem((HALO + TEAM, D), bf16),
            vmem((4, 3, D, CH), bf16),
            vmem((4 * CH, D), bf16),
            vmem((4, 64, CH), f32),
            vmem((3, 2, (LEAD + STEPS) * SEGS, 128), f32),
            vmem((2, TEAM, 128), f32),
            vmem((4, 2, TEAM, 128), f32),
            vmem((4, 2, TEAM, 128), f32),
            vmem((4, 2, POLES, SEGS, 128), f32),
            vmem((2, TEAM, 128), f32),
            vmem((4, TEAM, CH), bf16),
            vmem((TEAM, D), bf16),
            vmem((4, ROWS, D), bf16),
            vmem((4, 4, 2, POLES, 128), f32),
            vmem((8, 4, 2, POLES, 128), f32),
            vmem((4, 2, POLES, 128), f32),
            vmem((ROWS, D), bf16),
            pltpu.SemaphoreType.DMA((NSEM,)),
            pltpu.SemaphoreType.DMA((NSEM,)),
            pltpu.SemaphoreType.DMA((3, OUT_PARTS)),
            pltpu.SemaphoreType.DMA((3, OUT_PARTS)),
            pltpu.SemaphoreType.DMA((4,)),
        ],
        compiler_params=pltpu.CompilerParams(
            collective_id=0, has_side_effects=True, vmem_limit_bytes=62 * 1024 * 1024
        ),
    )(
        tokens,
        norm_gain.reshape(1, D),
        jnp.transpose(w_in, (1, 0, 2)),
        jnp.transpose(conv_w, (1, 0, 2)),
        decay_rate,
        residue,
        skip_gain.reshape(1, CH),
        w_out,
    )


def solution(mesh):
    return jax.shard_map(
        shards,
        mesh=mesh,
        in_specs=(
            P(("ctx", "tp"), None),
            P(),
            P(None, None, "tp"),
            P(None, None, "tp"),
            P(None, "tp"),
            P(None, "tp"),
            P("tp"),
            P("tp", None),
        ),
        out_specs=P(("ctx", "tp"), None),
        check_vma=False,
    )
```

time: 509 us -> 189 us (0.37)
  waiting for transfers between devices: 210 us -> 0 us
  Pallas kernels: 0 us -> 186 us
  local copies, waits for them, and re-layouts: 130 us -> 2.29 us
  matrix products: 65.7 us -> 0 us
  other arithmetic: 58.7 us -> 0 us
  blocking collectives: 25.1 us -> 0 us
  between operations: 13.7 us -> 0.01 us
    pallas_call x0 -> x1, Pallas kernels: none -> 186 us  [shards(): pl.pallas_call(kernel, out_shape=jax.ShapeDtypeStruct(tokens.shape, token...]
    reduce_scatter x1 -> x0, waiting for transfers between devices: 109 us -> none  [shards(): lax.psum_scatter(jnp.dot(gated, w_out, preferred_element_type=jnp.float32...]
    all_gather x1 -> x0, waiting for transfers between devices: 101 us -> none  [shards(): lax.all_gather(normed, 'tp', axis=0, tiled=True)]
    gather x2 -> x0, local copies, waits for them, and re-layouts: 79.7 us -> none  [channel_tables(): impulse[:, jnp.maximum(lag_rows, 0)]]
    dot_general x5 -> x0, matrix products: 65.7 us -> none  [the longest x1 28.9 us: long_mix(): within = jnp.einsum('cts,cbs->cbt', toeplitz, grouped, precision=highest)]
    add x13 -> x0, other arithmetic: 27.6 us -> none  [the longest x1 19.1 us: featurize(): summed + filter_taps[offset] * extended[..., offset:offset + length, :]]
    all_gather x2 -> x0, blocking collectives: 25.1 us -> none  [entering(): lax.all_gather(part.astype(kind), axis)]
    slice x7 -> x0, local copies, waits for them, and re-layouts: 18.9 us -> none  [the longest x5 18.8 us: block_states(): lax.associative_scan(combine_states, (block_decay, block_ends), axis=2)[1]]
  transfers between devices with their start and end apart: 3 -> 0, of which waited for: 2 -> 0; matrix products, arithmetic and copies ran while one was open for 18% -> 0% of each run, Pallas kernels for 0% -> 0%
where the time goes in v1:
time: 189 us; the launch traced here: 188 us
  Pallas kernels  186 us (98%)
  local copies, waits for them, and re-layouts  2.29 us (1%)
    pallas_call x1, Pallas kernels, shards(): pl.pallas_call(kernel, out_shape=jax.ShapeDtypeStruct(tokens.shape, token...  186 us

profile of v1, /device:TPU:1, one launch (start us, length us, event | category | flops | bytes accessed | tf_op | source)
XLA Modules:
  0.0 188.2 jit_solution(9646823643928870394)
XLA Ops:
  0.0 185.9 %shard_map.82 = bf16[128,4096]{1,0:T(8,128)(2,1)} custom-call(bf16[128,4096]{1,0:T(8,128)(2,1)} %tok_h.1, f32[1,4096]{1,0:T(1,128)} %bitcast.6, bf16[3,4096,256]{2,1,0:T(8,128)(2,1)} %bitcast.4, f32[3,7,256]{2,1,0:T(8,128)} %bitcast.5, f32[16,256]{1,0:T(8,128)} %decay.1, f32[16,256]{1,0:T(8,128)} %res.1, f32[1,256]{1,0:T(1,128)} %bitcast.7, ...), custom_call_target="tpu_custom_call" | custom-call | tf_op jit(solution)/shard_map/pallas_call | solution.py:510
  185.9 2.3 %copy.10 = bf16[128,4096]{1,0:T(8,128)(2,1)} copy(bf16[128,4096]{1,0:T(8,128)(2,1)} %shard_map.82) | data formatting | bytes 2097152

commit v2 on v1

--- a/solution.py
+++ b/solution.py
@@ -19,9 +19,10 @@
 LEAD = 8
 EPS = 1e-05
 MESH = pl.DeviceIdType.MESH
-NSEM = 96
+NSEM = 150
 OUT_COLS = 512
 OUT_PARTS = D // OUT_COLS
+HALF_COLS = D // 2
 
 f32 = jnp.float32
 bf16 = jnp.bfloat16
@@ -41,7 +42,7 @@
     tok_h, gain, win_h, conv, decay, res, skip, wout_h,
     out_h,
     tok, lhs, w_all, w_out, par, proj, prod, q_all, y_all, pref, gbuf, gated,
-    stage, landed, ends, totals, carry, outv, send, recv, osend, orecv, local,
+    stage, far, near, ends, totals, carry, outv, send, recv, osend, orecv, local,
 ):
     ctx = lax.axis_index("ctx")
     tp = lax.axis_index("tp")
@@ -110,13 +111,13 @@
         if kind == "in":
             return w_all.at[g, 1 + half, rows_in(zz)]
         at = g * CH + k * 128 + zz * 32 + half * 16
-        return w_out.at[pl.ds(pl.multiple_of(at, 16), 16)]
+        return w_out.at[pl.ds(pl.multiple_of(at, 16), 16), pl.ds(kind * HALF_COLS, HALF_COLS)]
 
     def own_piece(kind, half):
         if kind == "in":
             return win_h.at[1 + half, rows_in(z)]
         at = k * 128 + z * 32 + half * 16
-        return wout_h.at[pl.ds(pl.multiple_of(at, 16), 16)]
+        return wout_h.at[pl.ds(pl.multiple_of(at, 16), 16), pl.ds(kind * HALF_COLS, HALF_COLS)]
 
     class Weights:
         def __init__(self, kind):
@@ -127,33 +128,44 @@
             self.fwd_p = remote(piece(kind, gm, z, 0), piece(kind, gm, z, 0), YP)
             self.fwd_m = remote(piece(kind, gp, z, 1), piece(kind, gp, z, 1), YM)
             same = lambda g, zz, h, d: remote(piece(kind, g, zz, h), piece(kind, g, zz, h), d)
-            self.z_p, self.z_m, self.zf_p, self.zf_m = {}, {}, {}, {}
+            self.z_p, self.z_m, self.zf_p, self.zf_m, self.push = {}, {}, {}, {}, {}
             for name, g in (("m", gm), ("p", gp), ("2", g2)):
                 self.z_p[name] = [same(g, z, h, ZP) for h in range(2)]
                 self.z_m[name] = [same(g, z, h, ZM) for h in range(2)]
                 self.zf_p[name] = same(g, (z + 3) % 4, 0, ZP)
                 self.zf_m[name] = same(g, (z + 1) % 4, 1, ZM)
+                self.push[name] = {}
+                if kind == "in":
+                    for dz in range(4):
+                        for h in range(2):
+                            self.push[name][dz, h] = same(g, (z + dz) % 4, h, SIB)
 
         def start(self):
-            for h in (0, 1):
-                go(self.to_p[h] if h == 0 else self.to_m[h])
-                go(self.to_m[h] if h == 0 else self.to_p[h])
+            go(self.to_p[0])
+            go(self.to_m[1])
+            go(self.to_p[1])
+            go(self.to_m[0])
+
+        def share(self, name, dz, h):
+            if self.kind == "in":
+                go(self.push[name][dz, h])
 
         def spread(self, name, h):
             go(self.z_p[name][h])
             go(self.z_m[name][h])
+            self.share(name, 0, h)
 
         def along_y(self):
             self.to_p[0].wait_recv()
             go(self.fwd_p)
             self.spread("m", 0)
-            self.to_m[0].wait_recv()
-            self.spread("p", 0)
             self.to_m[1].wait_recv()
             go(self.fwd_m)
             self.spread("p", 1)
             self.to_p[1].wait_recv()
             self.spread("m", 1)
+            self.to_m[0].wait_recv()
+            self.spread("p", 0)
 
         def along_y2(self):
             self.fwd_p.wait_recv()
@@ -161,20 +173,40 @@
             self.fwd_m.wait_recv()
             self.spread("2", 1)
 
-        def forward_z(self, name):
+        def forward_p(self, name):
             self.z_p[name][0].wait_recv()
             go(self.zf_p[name])
+            self.share(name, 3, 0)
+
+        def forward_m(self, name):
             self.z_m[name][1].wait_recv()
             go(self.zf_m[name])
+            self.share(name, 1, 1)
+
+        def forward_z(self):
+            self.forward_p("m")
+            self.forward_m("p")
+            self.forward_m("m")
+            self.forward_p("p")
+
+        def finish_near(self, name):
+            self.z_m[name][0].wait_recv()
+            self.share(name, 1, 0)
+            self.z_p[name][1].wait_recv()
+            self.share(name, 3, 1)
+
+        def finish_far(self, name):
+            self.zf_p[name].wait_recv()
+            self.share(name, 2, 0)
+            self.zf_m[name].wait_recv()
+            self.share(name, 2, 1)
 
         def finish(self, name):
-            self.z_m[name][0].wait_recv()
-            self.z_p[name][1].wait_recv()
-            self.zf_p[name].wait_recv()
-            self.zf_m[name].wait_recv()
+            self.finish_near(name)
+            self.finish_far(name)
 
     wi = Weights("in")
-    wo = Weights("out")
+    wo = [Weights(0), Weights(1)]
 
     def q_rows(h):
         return pl.ds(pl.multiple_of(k * 2048 + h * 1024, 1024), 1024)
@@ -187,13 +219,18 @@
     q_fp = remote(w_all.at[gm, 0, q_rows(0)], w_all.at[gm, 0, q_rows(0)], YP)
     q_fm = remote(w_all.at[gp, 0, q_rows(1)], w_all.at[gp, 0, q_rows(1)], YM)
 
-    half = pl.ds(pl.multiple_of(k * 2048, 2048), 2048)
-    push = {}
+    q_push = {}
     push_out = {}
     for name, g in (("m", gm), ("p", gp), ("2", g2)):
-        push[name] = [remote(w_all.at[g, s, half], w_all.at[g, s, half], SIB) for s in range(3)]
+        q_push[name] = []
+        for h in range(2):
+            block = w_all.at[g, 0, q_rows(h)]
+            q_push[name].append(remote(block, block, SIB))
         o_half = pl.ds(pl.multiple_of(g * CH + k * 128, 128), 128)
-        push_out[name] = remote(w_out.at[o_half], w_out.at[o_half], SIB)
+        push_out[name] = []
+        for c in range(2):
+            block = w_out.at[o_half, pl.ds(c * HALF_COLS, HALF_COLS)]
+            push_out[name].append(remote(block, block, SIB))
 
     par_copies = [remote(par.at[y], par.at[y], dev(dy=d)) for d in (1, 3, 2)]
 
@@ -219,37 +256,40 @@
 
     lax.fori_loop(0, 4, norm_rows, 0)
     go(x_p[0])
-    go(x_m[0])
     lax.fori_loop(4, 8, norm_rows, 0)
     go(x_m[1])
     go(x_p[1])
-    for c in par_copies:
-        go(c)
+    go(x_m[0])
+
+    wi.along_y()
     go(q_p[0])
     go(q_m[1])
     go(q_m[0])
     go(q_p[1])
-
-    wi.along_y()
-    wi.along_y2()
     x_p[0].wait_recv()
     go(x_fp)
     x_m[1].wait_recv()
     go(x_fm)
-    wi.forward_z("m")
-    wi.forward_z("p")
+    wi.forward_p("m")
+    wi.forward_m("p")
+    for c in par_copies:
+        go(c)
+    wi.forward_m("m")
+    wi.forward_p("p")
+    wi.along_y2()
     q_p[0].wait_recv()
     go(q_fp)
+    go(q_push["m"][0])
     q_m[1].wait_recv()
     go(q_fm)
-    wo.start()
+    go(q_push["p"][1])
+    wi.finish_near("m")
+    wi.finish_near("p")
     x_p[1].wait_recv()
     x_m[0].wait_recv()
     x_fp.wait_recv()
     x_fm.wait_recv()
     go(halo_copy)
-    for c in par_copies:
-        c.wait_recv()
     copy_win.wait()
     halo_copy.wait_recv()
 
@@ -261,11 +301,7 @@
 
     def project(g):
         for s in range(3):
-            def k_step(j, acc):
-                at = pl.ds(pl.multiple_of(j * 1024, 1024), 1024)
-                return acc + jnp.dot(lhs[:, at], w_all[g, s, at, :], preferred_element_type=f32)
-
-            acc = lax.fori_loop(0, 4, k_step, jnp.zeros((HALO + TEAM, CH), f32))
+            acc = jnp.dot(lhs[...], w_all[g, s], preferred_element_type=f32)
             acc = acc.astype(bf16).astype(f32)
             for h in range(2):
                 part = acc[:, h * 128:(h + 1) * 128]
@@ -322,59 +358,70 @@
             states = lax.fori_loop(
                 0, STEPS // 4, steps, [jnp.zeros((SEGS, 128), f32)] * POLES
             )
+            last_rows = []
             for n in range(POLES):
                 v = states[n]
                 for dist in (1, 2, 4):
                     hop = jnp.exp(rate[n:n + 1] * (-1.0 * STEPS * dist))
                     v = v + hop * jnp.where(sub >= dist, pltpu.roll(v, dist, 0), 0.0)
                 pref[g, h, n] = jnp.where(sub >= 1, pltpu.roll(v, 1, 0), 0.0)
-                ends[y, g, h, n:n + 1, :] = v[SEGS - 1:SEGS]
-
-    def weights_ready(name):
-        wi.finish(name)
-        go(push[name][1])
-        go(push[name][2])
-
-    def q_ready(name):
-        if name == "m":
-            q_p[1].wait_recv()
-        elif name == "p":
-            q_m[0].wait_recv()
-        else:
-            q_fp.wait_recv()
-            q_fm.wait_recv()
-        go(push[name][0])
+                last_rows.append(v[SEGS - 1:SEGS])
+            ends[y, g, h] = jnp.concatenate(last_rows, axis=0).astype(bf16)
+
+    def shared(name):
+        for c in list(wi.push[name].values()) + q_push[name]:
+            c.wait_recv()
 
     def group(i, c):
         @pl.when(i == 1)
         def _():
-            wi.forward_z("2")
-            q_ready("m")
-            q_ready("p")
-            weights_ready("m")
-            wo.along_y()
-            weights_ready("p")
-            for c in push["m"]:
+            for c in par_copies:
                 c.wait_recv()
+            shared("m")
 
         @pl.when(i == 2)
         def _():
-            wo.along_y2()
-            q_ready("2")
-            for c in push["p"]:
-                c.wait_recv()
+            shared("p")
 
         @pl.when(i == 3)
         def _():
-            weights_ready("2")
-            wo.forward_z("m")
-            wo.forward_z("p")
-            for c in push["2"]:
-                c.wait_recv()
+            shared("2")
 
         turn = jnp.where(i == 0, 0, jnp.where(i == 1, 3, jnp.where(i == 2, 1, 2)))
         g = (y + turn) % 4
         project(g)
+
+        @pl.when(i == 0)
+        def _():
+            wi.forward_p("2")
+            wi.forward_m("2")
+            wi.finish_far("m")
+            q_p[1].wait_recv()
+            go(q_push["m"][1])
+            q_m[0].wait_recv()
+            go(q_push["p"][0])
+
+        @pl.when(i == 1)
+        def _():
+            wi.finish_far("p")
+            wi.finish_near("2")
+            wo[0].start()
+
+        @pl.when(i == 2)
+        def _():
+            q_fp.wait_recv()
+            go(q_push["2"][0])
+            q_fm.wait_recv()
+            go(q_push["2"][1])
+            wi.finish_far("2")
+            wo[0].along_y()
+
+        @pl.when(i == 3)
+        def _():
+            wo[0].along_y2()
+            wo[0].forward_z()
+            wo[1].start()
+
         featurize(g)
         scan(g)
         return c
@@ -384,17 +431,19 @@
     end_copies = [remote(ends.at[y], ends.at[y], dev(dy=d)) for d in (1, 3, 2)]
     for c in end_copies:
         go(c)
-    wo.forward_z("2")
+    wo[0].forward_p("2")
+    wo[0].forward_m("2")
+    wo[1].along_y()
     for c in end_copies:
         c.wait_recv()
     for g in range(4):
         for h in range(2):
             rate = par[g, 24:40, h * 128:(h + 1) * 128]
             hop = jnp.exp(rate * (-1.0 * TEAM))
-            total = ends[0, g, h]
+            total = ends[0, g, h].astype(f32)
             for yy in range(1, 4):
-                total = hop * total + ends[yy, g, h]
-            totals[ctx, g, h] = total
+                total = hop * total + ends[yy, g, h].astype(f32)
+            totals[ctx, g, h] = total.astype(bf16)
     total_copies = [
         remote(totals.at[ctx], totals.at[ctx], dev(dz=a, dk=b))
         for a in range(4) for b in range(2) if a or b
@@ -402,21 +451,23 @@
     for c in total_copies:
         go(c)
     for name in ("m", "p", "2"):
-        wo.finish(name)
-        go(push_out[name])
+        wo[0].finish(name)
+        go(push_out[name][0])
+    wo[1].along_y2()
+    wo[1].forward_z()
     for c in total_copies:
         c.wait_recv()
 
     for g in range(4):
         for h in range(2):
             rate = par[g, 24:40, h * 128:(h + 1) * 128]
-            far = jnp.exp(rate * (-4.0 * TEAM))
-            near = jnp.exp(rate * (-1.0 * TEAM))
+            shard_hop = jnp.exp(rate * (-4.0 * TEAM))
+            team_hop = jnp.exp(rate * (-1.0 * TEAM))
             v = jnp.zeros((POLES, 128), f32)
             for cc in range(7):
-                v = jnp.where(cc < ctx, far * v + totals[cc, g, h], v)
+                v = jnp.where(cc < ctx, shard_hop * v + totals[cc, g, h].astype(f32), v)
             for yy in range(3):
-                v = jnp.where(yy < y, near * v + ends[yy, g, h], v)
+                v = jnp.where(yy < y, team_hop * v + ends[yy, g, h].astype(f32), v)
             carry[g, h] = v
 
     segs = sub.astype(f32)
@@ -451,50 +502,85 @@
     lax.fori_loop(0, 4, correct, 0)
 
     copy_out.wait()
+    wo[1].forward_p("2")
+    wo[1].forward_m("2")
     for name in ("m", "p", "2"):
-        push_out[name].wait_recv()
-
-    def part_copy(n, d):
-        cols = pl.ds(pl.multiple_of(n * OUT_COLS, OUT_COLS), OUT_COLS)
-        to = (x + d) % 4
-        rows = pl.ds(pl.multiple_of(to * ROWS, ROWS), ROWS)
+        push_out[name][0].wait_recv()
+
+    def block_rows(who):
+        return pl.ds(pl.multiple_of((who % 4) * ROWS, ROWS), ROWS)
+
+    def part_cols(n):
+        return pl.ds(pl.multiple_of(n * OUT_COLS, OUT_COLS), OUT_COLS)
+
+    def side_cols(n, side):
+        width = OUT_COLS // 2
+        return pl.ds(pl.multiple_of(n * OUT_COLS + side * width, width), width)
+
+    def far_copy(n, side):
+        width = OUT_COLS // 2
         return pltpu.make_async_remote_copy(
-            src_ref=stage.at[rows, cols], dst_ref=landed.at[x, :, cols],
-            send_sem=osend.at[d - 1, n], recv_sem=orecv.at[d - 1, n],
-            device_id=dev(dx=d), device_id_type=MESH,
+            src_ref=stage.at[block_rows(x + 2), side_cols(n, side)],
+            dst_ref=far.at[side, :, pl.ds(pl.multiple_of(n * width, width), width)],
+            send_sem=osend.at[side, n], recv_sem=orecv.at[side, n],
+            device_id=XM if side else XP, device_id_type=MESH,
         )
 
+    def near_copy(n, side):
+        return pltpu.make_async_remote_copy(
+            src_ref=stage.at[block_rows(x + (3 if side else 1)), part_cols(n)],
+            dst_ref=near.at[side, :, part_cols(n)],
+            send_sem=osend.at[2 + side, n], recv_sem=orecv.at[2 + side, n],
+            device_id=XM if side else XP, device_id_type=MESH,
+        )
+
     def out_part(n, c):
-        cols = pl.ds(pl.multiple_of(n * OUT_COLS, OUT_COLS), OUT_COLS)
+        cols = part_cols(n)
         acc = jnp.zeros((TEAM, OUT_COLS), f32)
         for g in range(4):
             acc = acc + jnp.dot(gated[g], w_out[g * CH:(g + 1) * CH, cols], preferred_element_type=f32)
         stage[:, cols] = acc.astype(bf16)
-        for d in (2, 1, 3):
-            part_copy(n, d).start()
+        for side in range(2):
+            far_copy(n, side).start()
         return c
 
-    lax.fori_loop(0, OUT_PARTS, out_part, 0)
+    def pass_on(n, c):
+        width = OUT_COLS // 2
+        for side in range(2):
+            far_copy(n, side).wait_recv()
+            rows, cols = block_rows(x + (3 if side else 1)), side_cols(n, side)
+            came = far[side, :, pl.ds(pl.multiple_of(n * width, width), width)]
+            stage[rows, cols] = (stage[rows, cols].astype(f32) + came.astype(f32)).astype(bf16)
+            near_copy(n, side).start()
+        return c
 
     def add_part(n, c):
-        cols = pl.ds(pl.multiple_of(n * OUT_COLS, OUT_COLS), OUT_COLS)
-        for d in (1, 2, 3):
-            part_copy(n, d).wait_recv()
-        total = tok[:, cols].astype(f32) + stage[
-            pl.ds(pl.multiple_of(x * ROWS, ROWS), ROWS), cols
-        ].astype(f32)
-        for d in (1, 2, 3):
-            total = total + landed[(x + d) % 4, :, cols].astype(f32)
+        cols = part_cols(n)
+        for side in range(2):
+            near_copy(n, side).wait_recv()
+        total = tok[:, cols].astype(f32) + stage[block_rows(x), cols].astype(f32)
+        for side in range(2):
+            total = total + near[side, :, cols].astype(f32)
         outv[:, cols] = total.astype(bf16)
         return c
 
+    lax.fori_loop(0, OUT_PARTS // 2, out_part, 0)
+    for name in ("m", "p", "2"):
+        wo[1].finish(name)
+        go(push_out[name][1])
+    lax.fori_loop(0, OUT_PARTS // 2, pass_on, 0)
+    for name in ("m", "p", "2"):
+        push_out[name][1].wait_recv()
+    lax.fori_loop(OUT_PARTS // 2, OUT_PARTS, out_part, 0)
+    lax.fori_loop(OUT_PARTS // 2, OUT_PARTS, pass_on, 0)
     lax.fori_loop(0, OUT_PARTS, add_part, 0)
     copy_res = pltpu.make_async_copy(outv, out_h, local.at[3])
     copy_res.start()
 
     def sent_part(n, c):
-        for d in (1, 2, 3):
-            part_copy(n, d).wait_send()
+        for side in range(2):
+            far_copy(n, side).wait_send()
+            near_copy(n, side).wait_send()
         return c
 
     lax.fori_loop(0, OUT_PARTS, sent_part, 0)
@@ -526,15 +612,16 @@
             vmem((2, TEAM, 128), f32),
             vmem((4, TEAM, CH), bf16),
             vmem((TEAM, D), bf16),
-            vmem((4, ROWS, D), bf16),
-            vmem((4, 4, 2, POLES, 128), f32),
-            vmem((8, 4, 2, POLES, 128), f32),
+            vmem((2, ROWS, HALF_COLS), bf16),
+            vmem((2, ROWS, D), bf16),
+            vmem((4, 4, 2, POLES, 128), bf16),
+            vmem((8, 4, 2, POLES, 128), bf16),
             vmem((4, 2, POLES, 128), f32),
             vmem((ROWS, D), bf16),
             pltpu.SemaphoreType.DMA((NSEM,)),
             pltpu.SemaphoreType.DMA((NSEM,)),
-            pltpu.SemaphoreType.DMA((3, OUT_PARTS)),
-            pltpu.SemaphoreType.DMA((3, OUT_PARTS)),
+            pltpu.SemaphoreType.DMA((4, OUT_PARTS)),
+            pltpu.SemaphoreType.DMA((4, OUT_PARTS)),
             pltpu.SemaphoreType.DMA((4,)),
         ],
         compiler_params=pltpu.CompilerParams(

time: 189 us -> 157 us (0.83)
  Pallas kernels: 186 us -> 154 us
    pallas_call x1, Pallas kernels: 186 us -> 154 us  [shards(): pl.pallas_call(kernel, out_shape=jax.ShapeDtypeStruct(tokens.shape, token...]
where the time goes in v2:
time: 157 us
  Pallas kernels  154 us (98%)
  local copies, waits for them, and re-layouts  2.29 us (1%)
    pallas_call x1, Pallas kernels, shards(): pl.pallas_call(kernel, out_shape=jax.ShapeDtypeStruct(tokens.shape, token...  154 us

profile of v2, /device:TPU:1, one launch (start us, length us, event | category | flops | bytes accessed | tf_op | source)
XLA Modules:
  0.0 156.8 jit_solution(13207799724014456534)
XLA Ops:
  0.0 154.5 %shard_map.82 = bf16[128,4096]{1,0:T(8,128)(2,1)} custom-call(bf16[128,4096]{1,0:T(8,128)(2,1)} %tok_h.1, f32[1,4096]{1,0:T(1,128)} %bitcast.6, bf16[3,4096,256]{2,1,0:T(8,128)(2,1)} %bitcast.4, f32[3,7,256]{2,1,0:T(8,128)} %bitcast.5, f32[16,256]{1,0:T(8,128)} %decay.1, f32[16,256]{1,0:T(8,128)} %res.1, f32[1,256]{1,0:T(1,128)} %bitcast.7, ...), custom_call_target="tpu_custom_call" | custom-call | tf_op jit(solution)/shard_map/pallas_call | solution.py:596
  154.5 2.3 %copy.10 = bf16[128,4096]{1,0:T(8,128)(2,1)} copy(bf16[128,4096]{1,0:T(8,128)(2,1)} %shard_map.82) | data formatting | bytes 2097152

commit v3 on v2

--- a/solution.py
+++ b/solution.py
@@ -19,7 +19,7 @@
 LEAD = 8
 EPS = 1e-05
 MESH = pl.DeviceIdType.MESH
-NSEM = 150
+NSEM = 200
 OUT_COLS = 512
 OUT_PARTS = D // OUT_COLS
 HALF_COLS = D // 2
@@ -57,8 +57,6 @@
 
     place = ctx * 4 + y
     after, before = (place + 1) % 32, (place + 31) % 32
-    dev_after = (after // 4, (after % 4) * 4 + x)
-    dev_before = (before // 4, (before % 4) * 4 + x)
 
     count = [0]
     started = []
@@ -77,6 +75,13 @@
         return copy
 
     gm, gp, g2 = (y + 3) % 4, (y + 1) % 4, (y + 2) % 4
+
+    partners = [dev(dx=1), dev(dx=2), dev(dx=3), dev(dy=1), dev(dy=2), dev(dy=3)]
+    partners += [dev(dz=a, dk=b) for a in range(4) for b in range(2) if a or b]
+    halo_from = (before // 4, (before % 4) * 4 + 3)
+    barrier = pltpu.get_barrier_semaphore()
+    for d in partners + [halo_from]:
+        pl.semaphore_signal(barrier, inc=1, device_id=d, device_id_type=MESH)
 
     copy_tok = pltpu.make_async_copy(tok_h, tok, local.at[0])
     copy_win = pltpu.make_async_copy(win_h, w_all.at[y], local.at[1])
@@ -87,37 +92,41 @@
     copy_win.start()
     copy_out.start()
 
+
     for s in range(3):
         par[y, s * 8:s * 8 + TAPS, :] = conv[s]
     par[y, 24:40, :] = decay[...]
     par[y, 40:56, :] = res[...]
     par[y, 56:57, :] = skip[...]
 
-    partners = [dev(dx=1), dev(dx=2), dev(dx=3), dev(dy=1), dev(dy=2), dev(dy=3)]
-    partners += [dev(dz=a, dk=b) for a in range(4) for b in range(2) if a or b]
-    partners += [dev_after, dev_before]
-    barrier = pltpu.get_barrier_semaphore()
-    for d in partners:
-        pl.semaphore_signal(barrier, inc=1, device_id=d, device_id_type=MESH)
-    pl.semaphore_wait(barrier, len(partners))
+    def norm_rows(i, c):
+        v = tok[pl.ds(pl.multiple_of(i * 16, 16), 16), :].astype(f32)
+        ms = jnp.sum(v * v, axis=1, keepdims=True) * (1.0 / D)
+        v = (v * lax.rsqrt(ms + EPS) * gain[...]).astype(bf16)
+        lhs[pl.ds(pl.multiple_of(HALO + x * ROWS + i * 16, 16), 16), :] = v
+        return c
+
+    copy_tok.wait()
+    lax.fori_loop(0, ROWS // 16, norm_rows, 0)
+    pl.semaphore_wait(barrier, len(partners) + jnp.where(x == 3, 4, 0))
 
     YP, YM, ZP, ZM, SIB = dev(dy=1), dev(dy=3), dev(dz=1), dev(dz=3), dev(dk=1)
     XP, XM = dev(dx=1), dev(dx=3)
 
-    def rows_in(zz, n=512):
-        return pl.ds(pl.multiple_of(k * 2048 + zz * n, n), n)
-
-    def piece(kind, g, zz, half):
-        if kind == "in":
-            return w_all.at[g, 1 + half, rows_in(zz)]
-        at = g * CH + k * 128 + zz * 32 + half * 16
-        return w_out.at[pl.ds(pl.multiple_of(at, 16), 16), pl.ds(kind * HALF_COLS, HALF_COLS)]
-
-    def own_piece(kind, half):
-        if kind == "in":
-            return win_h.at[1 + half, rows_in(z)]
-        at = k * 128 + z * 32 + half * 16
-        return wout_h.at[pl.ds(pl.multiple_of(at, 16), 16), pl.ds(kind * HALF_COLS, HALF_COLS)]
+    def share_rows(zz, h):
+        return pl.ds(pl.multiple_of(k * 2048 + zz * 512 + h * 256, 256), 256)
+
+    def piece(kind, g, zz, h):
+        if kind != "out":
+            return w_all.at[g, kind, share_rows(zz, h)]
+        at = g * CH + k * 128 + zz * 32 + h * 16
+        return w_out.at[pl.ds(pl.multiple_of(at, 16), 16), pl.ds(HALF_COLS, HALF_COLS)]
+
+    def own_piece(kind, h):
+        if kind != "out":
+            return win_h.at[kind, share_rows(z, h)]
+        at = k * 128 + z * 32 + h * 16
+        return wout_h.at[pl.ds(pl.multiple_of(at, 16), 16), pl.ds(HALF_COLS, HALF_COLS)]
 
     class Weights:
         def __init__(self, kind):
@@ -135,7 +144,7 @@
                 self.zf_p[name] = same(g, (z + 3) % 4, 0, ZP)
                 self.zf_m[name] = same(g, (z + 1) % 4, 1, ZM)
                 self.push[name] = {}
-                if kind == "in":
+                if kind != "out":
                     for dz in range(4):
                         for h in range(2):
                             self.push[name][dz, h] = same(g, (z + dz) % 4, h, SIB)
@@ -147,7 +156,7 @@
             go(self.to_m[0])
 
         def share(self, name, dz, h):
-            if self.kind == "in":
+            if self.kind != "out":
                 go(self.push[name][dz, h])
 
         def spread(self, name, h):
@@ -201,36 +210,77 @@
             self.zf_m[name].wait_recv()
             self.share(name, 2, 1)
 
+        def shared(self, name):
+            for c in self.push[name].values():
+                c.wait_recv()
+
         def finish(self, name):
             self.finish_near(name)
             self.finish_far(name)
 
-    wi = Weights("in")
-    wo = [Weights(0), Weights(1)]
-
-    def q_rows(h):
-        return pl.ds(pl.multiple_of(k * 2048 + h * 1024, 1024), 1024)
-
-    def q_own(h, d):
-        return remote(win_h.at[0, q_rows(h)], w_all.at[y, 0, q_rows(h)], d)
-
-    q_p = [q_own(h, YP) for h in range(2)]
-    q_m = [q_own(h, YM) for h in range(2)]
-    q_fp = remote(w_all.at[gm, 0, q_rows(0)], w_all.at[gm, 0, q_rows(0)], YP)
-    q_fm = remote(w_all.at[gp, 0, q_rows(1)], w_all.at[gp, 0, q_rows(1)], YM)
-
-    q_push = {}
+    def line(kind, g, h):
+        if kind != "out":
+            return w_all.at[g, kind, pl.ds(pl.multiple_of(k * 2048 + h * 1024, 1024), 1024)]
+        at = g * CH + k * 128 + h * 64
+        return w_out.at[pl.ds(pl.multiple_of(at, 64), 64), pl.ds(0, HALF_COLS)]
+
+    def own_line(kind, h):
+        if kind != "out":
+            return win_h.at[kind, pl.ds(pl.multiple_of(k * 2048 + h * 1024, 1024), 1024)]
+        at = k * 128 + h * 64
+        return wout_h.at[pl.ds(pl.multiple_of(at, 64), 64), pl.ds(0, HALF_COLS)]
+
+    class Lines:
+        def __init__(self, kind):
+            self.to_p = [remote(own_line(kind, h), line(kind, y, h), YP) for h in range(2)]
+            self.to_m = [remote(own_line(kind, h), line(kind, y, h), YM) for h in range(2)]
+            same = lambda g, h, d: remote(line(kind, g, h), line(kind, g, h), d)
+            self.fwd_p = same(gm, 0, YP)
+            self.fwd_m = same(gp, 1, YM)
+            self.push = {
+                name: [same(g, h, SIB) for h in range(2)]
+                for name, g in (("m", gm), ("p", gp), ("2", g2))
+            }
+
+        def start_first(self):
+            go(self.to_p[0])
+            go(self.to_m[1])
+
+        def start_second(self):
+            go(self.to_p[1])
+            go(self.to_m[0])
+
+        def forward(self):
+            self.to_p[0].wait_recv()
+            go(self.fwd_p)
+            go(self.push["m"][0])
+            self.to_m[1].wait_recv()
+            go(self.fwd_m)
+            go(self.push["p"][1])
+
+        def near(self):
+            self.to_p[1].wait_recv()
+            go(self.push["m"][1])
+            self.to_m[0].wait_recv()
+            go(self.push["p"][0])
+
+        def far(self):
+            self.fwd_p.wait_recv()
+            go(self.push["2"][0])
+            self.fwd_m.wait_recv()
+            go(self.push["2"][1])
+
+        def shared(self, name):
+            for c in self.push[name]:
+                c.wait_recv()
+
+    wk, wv, wq = Weights(1), Lines(2), Weights(0)
+    wa, wb = Weights("out"), Lines("out")
     push_out = {}
     for name, g in (("m", gm), ("p", gp), ("2", g2)):
-        q_push[name] = []
-        for h in range(2):
-            block = w_all.at[g, 0, q_rows(h)]
-            q_push[name].append(remote(block, block, SIB))
         o_half = pl.ds(pl.multiple_of(g * CH + k * 128, 128), 128)
-        push_out[name] = []
-        for c in range(2):
-            block = w_out.at[o_half, pl.ds(c * HALF_COLS, HALF_COLS)]
-            push_out[name].append(remote(block, block, SIB))
+        block = w_out.at[o_half, pl.ds(HALF_COLS, HALF_COLS)]
+        push_out[name] = remote(block, block, SIB)
 
     par_copies = [remote(par.at[y], par.at[y], dev(dy=d)) for d in (1, 3, 2)]
 
@@ -242,56 +292,55 @@
     xm, xp = (x + 3) % 4, (x + 1) % 4
     x_fp = remote(x_rows(xm, 0), x_rows(xm, 0), XP)
     x_fm = remote(x_rows(xp, 1), x_rows(xp, 1), XM)
-    halo_copy = remote(lhs.at[pl.ds(TEAM, HALO)], lhs.at[pl.ds(0, HALO)], dev_after)
-
-    wi.start()
-    copy_tok.wait()
-
-    def norm_rows(i, c):
-        v = tok[pl.ds(pl.multiple_of(i * 16, 16), 16), :].astype(f32)
-        ms = jnp.sum(v * v, axis=1, keepdims=True) * (1.0 / D)
-        v = (v * lax.rsqrt(ms + EPS) * gain[...]).astype(bf16)
-        lhs[pl.ds(pl.multiple_of(HALO + x * ROWS + i * 16, 16), 16), :] = v
-        return c
-
-    lax.fori_loop(0, 4, norm_rows, 0)
+    halo_copies = [
+        pltpu.make_async_remote_copy(
+            src_ref=lhs.at[pl.ds(TEAM, HALO)], dst_ref=lhs.at[pl.ds(0, HALO)],
+            send_sem=send.at[NSEM - 1 - d], recv_sem=recv.at[NSEM - 1],
+            device_id=(after // 4, (after % 4) * 4 + d), device_id_type=MESH,
+        )
+        for d in range(4)
+    ]
+
+    @pl.when(x == 3)
+    def _():
+        for c in halo_copies:
+            c.start()
+
+    wk.start()
     go(x_p[0])
-    lax.fori_loop(4, 8, norm_rows, 0)
     go(x_m[1])
     go(x_p[1])
     go(x_m[0])
-
-    wi.along_y()
-    go(q_p[0])
-    go(q_m[1])
-    go(q_m[0])
-    go(q_p[1])
+    wk.along_y()
+    for c in par_copies:
+        go(c)
+    wq.start()
+    wv.start_first()
+    wv.start_second()
     x_p[0].wait_recv()
     go(x_fp)
     x_m[1].wait_recv()
     go(x_fm)
-    wi.forward_p("m")
-    wi.forward_m("p")
-    for c in par_copies:
-        go(c)
-    wi.forward_m("m")
-    wi.forward_p("p")
-    wi.along_y2()
-    q_p[0].wait_recv()
-    go(q_fp)
-    go(q_push["m"][0])
-    q_m[1].wait_recv()
-    go(q_fm)
-    go(q_push["p"][1])
-    wi.finish_near("m")
-    wi.finish_near("p")
+    wk.forward_p("m")
+    wk.forward_m("p")
+    wk.forward_m("m")
+    wk.forward_p("p")
+    wk.along_y2()
+    wq.along_y()
+    wv.forward()
+    wq.along_y2()
+    wk.finish_near("m")
+    wk.finish_near("p")
+    wk.forward_p("2")
+    wk.forward_m("2")
+    wk.finish_far("m")
+    wk.finish_far("p")
     x_p[1].wait_recv()
     x_m[0].wait_recv()
     x_fp.wait_recv()
     x_fm.wait_recv()
-    go(halo_copy)
     copy_win.wait()
-    halo_copy.wait_recv()
+    halo_copies[0].wait_recv()
 
     @pl.when(place == 0)
     def _():
@@ -299,8 +348,8 @@
 
     sub = lax.broadcasted_iota(jnp.int32, (SEGS, 128), 0)
 
-    def project(g):
-        for s in range(3):
+    def project(g, streams):
+        for s in streams:
             acc = jnp.dot(lhs[...], w_all[g, s], preferred_element_type=f32)
             acc = acc.astype(bf16).astype(f32)
             for h in range(2):
@@ -316,22 +365,24 @@
                         sub == 0, first, pltpu.roll(last, 1, 0)
                     )
 
-    def featurize(g):
+    def featurize(g, streams):
         for h in range(2):
             lanes = pl.ds(h * 128, 128)
             taps = [par[g, s * 8:s * 8 + 8, lanes] for s in range(3)]
 
             def steps(i, c):
                 feats = []
-                for s in range(3):
+                for s in streams:
                     at = pl.multiple_of((i * 8 + LEAD - TAPS + 1) * SEGS, SEGS)
                     rows = proj[s, h, pl.ds(at, 14 * SEGS), :]
                     feats.append(tree_sum([
                         taps[s][j:j + 1] * rows[j * SEGS:j * SEGS + 64] for j in range(TAPS)
                     ]))
                 to = pl.ds(pl.multiple_of(i * 64, 64), 64)
-                q_all[g, h, to, :] = feats[0]
-                prod[h, to, :] = feats[1] * feats[2]
+                if len(feats) == 2:
+                    prod[h, to, :] = feats[0] * feats[1]
+                else:
+                    q_all[g, h, to, :] = feats[0]
                 return c
 
             lax.fori_loop(0, STEPS // 8, steps, 0)
@@ -368,72 +419,71 @@
                 last_rows.append(v[SEGS - 1:SEGS])
             ends[y, g, h] = jnp.concatenate(last_rows, axis=0).astype(bf16)
 
-    def shared(name):
-        for c in list(wi.push[name].values()) + q_push[name]:
-            c.wait_recv()
-
     def group(i, c):
         @pl.when(i == 1)
         def _():
             for c in par_copies:
                 c.wait_recv()
-            shared("m")
+            wk.shared("m")
+            wv.shared("m")
 
         @pl.when(i == 2)
         def _():
-            shared("p")
+            wk.shared("p")
+            wv.shared("p")
 
         @pl.when(i == 3)
         def _():
-            shared("2")
+            wk.shared("2")
+            wv.shared("2")
 
         turn = jnp.where(i == 0, 0, jnp.where(i == 1, 3, jnp.where(i == 2, 1, 2)))
         g = (y + turn) % 4
-        project(g)
+        project(g, (1, 2))
 
         @pl.when(i == 0)
         def _():
-            wi.forward_p("2")
-            wi.forward_m("2")
-            wi.finish_far("m")
-            q_p[1].wait_recv()
-            go(q_push["m"][1])
-            q_m[0].wait_recv()
-            go(q_push["p"][0])
+            wk.finish_near("2")
+            wk.finish_far("2")
+            wv.near()
+            wa.start()
+            wb.start_first()
+            wb.start_second()
 
         @pl.when(i == 1)
         def _():
-            wi.finish_far("p")
-            wi.finish_near("2")
-            wo[0].start()
+            wq.forward_z()
 
         @pl.when(i == 2)
         def _():
-            q_fp.wait_recv()
-            go(q_push["2"][0])
-            q_fm.wait_recv()
-            go(q_push["2"][1])
-            wi.finish_far("2")
-            wo[0].along_y()
+            wv.far()
+            wq.finish_near("m")
+            wq.finish_near("p")
+            wa.along_y()
 
         @pl.when(i == 3)
         def _():
-            wo[0].along_y2()
-            wo[0].forward_z()
-            wo[1].start()
-
-        featurize(g)
+            wb.forward()
+            wq.forward_p("2")
+            wq.forward_m("2")
+            wq.finish_far("m")
+            wq.finish_far("p")
+            wa.along_y2()
+
+        featurize(g, (1, 2))
         scan(g)
         return c
 
     lax.fori_loop(0, 4, group, 0)
+
+    def gate_of(g):
+        project(g, (0,))
+        featurize(g, (0,))
 
     end_copies = [remote(ends.at[y], ends.at[y], dev(dy=d)) for d in (1, 3, 2)]
     for c in end_copies:
         go(c)
-    wo[0].forward_p("2")
-    wo[0].forward_m("2")
-    wo[1].along_y()
+    gate_of(y)
     for c in end_copies:
         c.wait_recv()
     for g in range(4):
@@ -450,11 +500,15 @@
     ]
     for c in total_copies:
         go(c)
-    for name in ("m", "p", "2"):
-        wo[0].finish(name)
-        go(push_out[name][0])
-    wo[1].along_y2()
-    wo[1].forward_z()
+    wq.shared("m")
+    gate_of(gm)
+    wq.finish("2")
+    wq.shared("p")
+    gate_of(gp)
+    wa.forward_z()
+    wb.near()
+    wq.shared("2")
+    gate_of(g2)
     for c in total_copies:
         c.wait_recv()
 
@@ -499,13 +553,14 @@
                 ].astype(bf16)
         return c
 
+    wa.forward_p("2")
+    wa.forward_m("2")
+    wb.far()
     lax.fori_loop(0, 4, correct, 0)
 
     copy_out.wait()
-    wo[1].forward_p("2")
-    wo[1].forward_m("2")
     for name in ("m", "p", "2"):
-        push_out[name][0].wait_recv()
+        wb.shared(name)
 
     def block_rows(who):
         return pl.ds(pl.multiple_of((who % 4) * ROWS, ROWS), ROWS)
@@ -566,11 +621,11 @@
 
     lax.fori_loop(0, OUT_PARTS // 2, out_part, 0)
     for name in ("m", "p", "2"):
-        wo[1].finish(name)
-        go(push_out[name][1])
+        wa.finish(name)
+        go(push_out[name])
     lax.fori_loop(0, OUT_PARTS // 2, pass_on, 0)
     for name in ("m", "p", "2"):
-        push_out[name][1].wait_recv()
+        push_out[name].wait_recv()
     lax.fori_loop(OUT_PARTS // 2, OUT_PARTS, out_part, 0)
     lax.fori_loop(OUT_PARTS // 2, OUT_PARTS, pass_on, 0)
     lax.fori_loop(0, OUT_PARTS, add_part, 0)
@@ -584,6 +639,11 @@
         return c
 
     lax.fori_loop(0, OUT_PARTS, sent_part, 0)
+    @pl.when(x == 3)
+    def _():
+        for c in halo_copies:
+            c.wait_send()
+
     for c in started:
         c.wait_send()
     copy_res.wait()

time: 157 us -> 145 us (0.924)
  Pallas kernels: 154 us -> 143 us
    pallas_call x1, Pallas kernels: 154 us -> 143 us  [shards(): pl.pallas_call(kernel, out_shape=jax.ShapeDtypeStruct(tokens.shape, token...]
where the time goes in v3:
time: 145 us
  Pallas kernels  143 us (99%)
  local copies, waits for them, and re-layouts  2.29 us (2%)
    pallas_call x1, Pallas kernels, shards(): pl.pallas_call(kernel, out_shape=jax.ShapeDtypeStruct(tokens.shape, token...  143 us

profile of v3, /device:TPU:1, one launch (start us, length us, event | category | flops | bytes accessed | tf_op | source)
XLA Modules:
  0.0 145.2 jit_solution(8162965093726024512)
XLA Ops:
  0.0 143.0 %shard_map.82 = bf16[128,4096]{1,0:T(8,128)(2,1)} custom-call(bf16[128,4096]{1,0:T(8,128)(2,1)} %tok_h.1, f32[1,4096]{1,0:T(1,128)} %bitcast.6, bf16[3,4096,256]{2,1,0:T(8,128)(2,1)} %bitcast.4, f32[3,7,256]{2,1,0:T(8,128)} %bitcast.5, f32[16,256]{1,0:T(8,128)} %decay.1, f32[16,256]{1,0:T(8,128)} %res.1, f32[1,256]{1,0:T(1,128)} %bitcast.7, ...), custom_call_target="tpu_custom_call" | custom-call | tf_op jit(solution)/shard_map/pallas_call | solution.py:656
  143.0 2.3 %copy.10 = bf16[128,4096]{1,0:T(8,128)(2,1)} copy(bf16[128,4096]{1,0:T(8,128)(2,1)} %shard_map.82) | data formatting | bytes 2097152
